TPU v7x, 32 devices: a whole 2x2x4 slice. The times are simulated.
32 devices in a mesh: head: 8 (over y, x, core), ctx: 4 (over z).
Axes of the slice: x: 2, y: 2, z: 4, core: 2. Of those that a mesh axis runs over, the one named last changes fastest.
Arguments:
- queries: bfloat16 [16384, 2048], P(('ctx', 'head')), may hold values from -20 to 20
- key_rows: bfloat16 [16384, 2048], P(('ctx', 'head')), may hold values from -20 to 20
- value_rows: bfloat16 [16384, 2048], P(('ctx', 'head')), may hold values from -6 to 6
- band_blocks: int32 [16], P('head'), may hold values from 1 to 4, as said below
- global_list: int32 [128, 8], P('ctx'), may hold values from -1 to 119, as said below
Outputs:
- attended: bfloat16 [16384, 2048], P(('ctx', 'head'))
Inputs may be any that keep to these rules, and one draw needn't show every extreme that they name: `global_list`: each entry is -1 or a key block j with j % 4 == 3 and j <= b - 5 for its row's query block b. A row's entries other than -1 are distinct and come first, the first being the largest such j, and a row holds min(8, the number of such j) of them. `band_blocks`: every value from 1 to 4 is taken by some head.
All inputs are finite; a program needn't handle non-finite values.
Results may differ from a plain program's by a relative error of at most 0.008.
Values may be sent and summed in bfloat16 or wider, within the bound.
A program may use at most 64 MiB of HBM per device.

v0:
```python
import jax
import jax.numpy as jnp
from jax import lax
from jax.sharding import PartitionSpec as P

HEAD_FEATURES = 128
BLOCK = 128
BAND_MAX = 4
STRIDE = 4
G = 8


def passed_along(array, axis, by):
    size = lax.axis_size(axis)
    pairs = [(i, i + by) for i in range(size) if 0 <= i + by < size]
    return lax.ppermute(array, axis, pairs)


def band_mask(first_block, group_size, reach_blocks):
    key_index = jnp.arange((BAND_MAX + 1) * BLOCK, dtype=jnp.int32)
    offset = key_index // BLOCK
    query_block = first_block + jnp.arange(group_size, dtype=jnp.int32)
    key_pos = (query_block[:, None] - BAND_MAX + offset[None, :]) * BLOCK + key_index[
        None, :
    ] % BLOCK
    query_pos = query_block[:, None] * BLOCK + jnp.arange(BLOCK, dtype=jnp.int32)[None, :]
    causal = (key_pos[:, None, :] >= 0) & (key_pos[:, None, :] <= query_pos[:, :, None])
    within = offset[None, :] >= BAND_MAX - reach_blocks[:, None]
    return causal[:, None, :, :] & within[None, :, None, :]


def global_mask(listed):
    return jnp.repeat(listed >= 0, BLOCK, axis=1)[:, None, None, :]


def scores_of(query_group, key_group):
    return jnp.einsum(
        "bqhd,bkhd->bhqk", query_group, key_group, preferred_element_type=jnp.float32
    ) * HEAD_FEATURES ** (-0.5)


def band_window(extended, start_block, group_size):
    window_rows = lax.dynamic_slice_in_dim(extended, start_block, group_size + BAND_MAX, 1)
    shifted = [window_rows[:, offset : offset + group_size] for offset in range(BAND_MAX + 1)]
    window = jnp.stack(shifted, axis=2)
    return window.reshape(2, group_size, (BAND_MAX + 1) * BLOCK, window.shape[4], HEAD_FEATURES)


def local(queries, key_rows, value_rows, band_blocks, global_list):
    heads_axis = lax.axis_size("head")
    feat_width = queries.shape[1] // heads_axis
    heads_here = feat_width // HEAD_FEATURES
    combined = lax.all_to_all(
        jnp.stack([queries, key_rows, value_rows]), "head", split_axis=2, concat_axis=1, tiled=True
    )
    keyval = combined[1:]
    length = keyval.shape[1]
    nblocks = length // BLOCK
    rim_rows = passed_along(keyval[:, length - BAND_MAX * BLOCK :], "ctx", 1)
    candidates = keyval.reshape(2, nblocks // STRIDE, STRIDE, BLOCK, feat_width)[:, :, STRIDE - 1]
    gathered = lax.all_gather(candidates, "ctx", axis=1, tiled=True)
    query_all = combined[0]
    group_size = min(4, nblocks)
    ngroups = nblocks // group_size
    first_global = lax.axis_index("ctx") * nblocks
    extended = jnp.concatenate([rim_rows, keyval], axis=1).reshape(
        2, nblocks + BAND_MAX, BLOCK, heads_here, HEAD_FEATURES
    )
    query_groups = query_all.reshape(ngroups, group_size, BLOCK, heads_here, HEAD_FEATURES)
    list_groups = global_list.reshape(ngroups, group_size, G)
    starts = jnp.arange(ngroups, dtype=jnp.int32) * group_size

    def attend_group(operands):
        query_group, listed, start_block = operands
        window = band_window(extended, start_block, group_size)
        band_ok = band_mask(first_global + start_block, group_size, band_blocks)
        picked = gathered[:, jnp.maximum(listed, 0) // STRIDE].reshape(
            2, group_size, G * BLOCK, heads_here, HEAD_FEATURES
        )
        logit_matrix = jnp.concatenate(
            [scores_of(query_group, window[0]), scores_of(query_group, picked[0])], axis=-1
        )
        listed_ok = jnp.broadcast_to(
            global_mask(listed), (group_size, heads_here, BLOCK, G * BLOCK)
        )
        allowed = jnp.concatenate([band_ok, listed_ok], axis=-1)
        every_value_row = jnp.concatenate([window[1], picked[1]], axis=1)
        row_top = jnp.max(jnp.where(allowed, logit_matrix, -1e30), axis=-1, keepdims=True)
        weights_raw = jnp.where(allowed, jnp.exp(logit_matrix - row_top), 0.0)
        row_weight_sum = jnp.sum(weights_raw, axis=-1)
        blended_output = jnp.einsum(
            "bhqk,bkhd->bhqd",
            weights_raw.astype(jnp.bfloat16),
            every_value_row,
            preferred_element_type=jnp.float32,
        )
        return (blended_output / row_weight_sum[..., None]).astype(jnp.bfloat16)

    result = lax.map(attend_group, (query_groups, list_groups, starts))
    attended = jnp.transpose(result, (0, 1, 3, 2, 4)).reshape(length, feat_width)
    return lax.all_to_all(attended, "head", split_axis=0, concat_axis=1, tiled=True)


def solution(mesh):
    in_specs = (
        P(("ctx", "head"), None),
        P(("ctx", "head"), None),
        P(("ctx", "head"), None),
        P("head"),
        P("ctx", None),
    )
    out_specs = P(("ctx", "head"), None)
    return jax.shard_map(local, mesh=mesh, in_specs=in_specs, out_specs=out_specs, check_vma=False)
```

profile of v0, /device:TPU:16, one launch (start us, length us, event | category | flops | bytes accessed | tf_op | source)
XLA Modules:
  0.0 679.3 jit_solution(4665914306781967896)
XLA Ops:
  6.5 6.4 pad_maximum_fusion.2
  12.9 14.1 %copy.59 = bf16[3,512,2048]{1,0,2:T(4,128)(2,1)} copy(bf16[3,512,2048]{2,1,0:T(8,128)(2,1)} %pad_maximum_fusion.2) | data formatting | bytes 12582912 | tf_op jit(solution)/shard_map/stack | solution.py:54
  27.0 97.8 %all_to_all.34 = bf16[3,512,2048]{1,0,2:T(4,128)(2,1)S(1)} all-to-all(bf16[3,512,2048]{1,0,2:T(4,128)(2,1)} %copy.59), channel_id=1, replica_groups=mesh['head'=8,'ctx'=4] {'head'}, dimensions={2} | all-to-all | bytes 12582912 | tf_op jit(solution)/shard_map/all_to_all | solution.py:53
  124.8 4.2 copy.60
  129.1 4.6 slice.95
  133.7 6.2 copy.62
  143.3 3.7 collective-permute-start
  151.1 23.6 %collective-permute-done = bf16[2,512,256]{2,1,0:T(8,128)(2,1)S(1)} collective-permute-done((bf16[2,512,256]{2,1,0:T(8,128)(2,1)S(1)}, bf16[2,512,256]{2,1,0:T(8,128)(2,1)S(1)}, u32[]{:S(2)}, u32[]{:S(2)}) %collective-permute-start) | collective-permute-done | bytes 524320 | tf_op jit(solution)/shard_map/ppermute | solution.py:16
  174.7 4.7 pad_maximum_fusion.3
  179.4 7.7 %reshape.265 = bf16[2,36,128,2,128]{4,3,2,1,0:T(2,128)(2,1)} reshape(bf16[2,4608,256]{2,1,0:T(8,128)(2,1)} %pad_maximum_fusion.3) | data formatting | bytes 9437184 | tf_op jit(solution)/shard_map/reshape | solution.py:66
  187.1 36.5 %all-gather.3.cloned.1.call-done = bf16[2,32,1,128,256]{4,3,2,1,0:T(8,128)(2,1)} async-done(((bf16[2,8,1,128,256]{4,3,2,1,0:T(8,128)(2,1)}), bf16[2,32,1,128,256]{4,3,2,1,0:T(8,128)(2,1)}) %all-gather.3.cloned.1.call-update) | async-done | bytes 4194320 | tf_op jit(solution)/shard_map/all_gather | solution.py:61
  223.6 406.1 %while.13 = (s32[]{:T(128)}, bf16[8,4,2,128,128]{4,3,2,1,0:T(8,128)(2,1)}, s32[8]{0:T(128)S(1)}, s32[]{:T(128)}, s32[2]{0:T(128)S(1)}, /*index=5*/s32[8,4,8]{2,1...) while((s32[]{:T(128)}, ...), condition=%wide.region_3.4_spmd, body=%wide.region_0.3_spmd.sunk | while | flops 897873664 | bytes 111360944 | solution.py:99
  226.2 4.2 constant_dynamic-slice_fusion.9
  237.6 4.9 gather_fusion
  242.5 7.5 %copy.113 = bf16[4,8,2,128,256]{3,1,4,0,2:T(8,128)(2,1)} copy(bf16[4,8,2,128,256]{4,3,2,1,0:T(8,128)(2,1)} %bitcast.118) | data formatting | bytes 8388608 | tf_op jit(solution)/shard_map/while/body/eval_jaxpr/gather | solution.py:77
  250.1 4.5 fusion.80
  254.5 2.8 squeeze.57
  259.6 3.9 fusion.89
  270.1 4.4 fusion.90
  277.0 4.2 constant_dynamic-slice_fusion.9
  288.4 4.9 gather_fusion
  293.4 7.5 %copy.113 = bf16[4,8,2,128,256]{3,1,4,0,2:T(8,128)(2,1)} copy(bf16[4,8,2,128,256]{4,3,2,1,0:T(8,128)(2,1)} %bitcast.118) | data formatting | bytes 8388608 | tf_op jit(solution)/shard_map/while/body/eval_jaxpr/gather | solution.py:77
  300.9 4.5 fusion.80
  310.4 3.9 fusion.89
  320.9 4.4 fusion.90
  327.8 4.1 constant_dynamic-slice_fusion.9
  339.2 4.9 gather_fusion
  344.1 7.5 %copy.113 = bf16[4,8,2,128,256]{3,1,4,0,2:T(8,128)(2,1)} copy(bf16[4,8,2,128,256]{4,3,2,1,0:T(8,128)(2,1)} %bitcast.118) | data formatting | bytes 8388608 | tf_op jit(solution)/shard_map/while/body/eval_jaxpr/gather | solution.py:77
  351.6 4.5 fusion.80
  361.2 3.9 fusion.89
  371.7 4.4 fusion.90
  378.6 4.0 constant_dynamic-slice_fusion.9
  389.9 4.9 gather_fusion
  394.8 7.5 %copy.113 = bf16[4,8,2,128,256]{3,1,4,0,2:T(8,128)(2,1)} copy(bf16[4,8,2,128,256]{4,3,2,1,0:T(8,128)(2,1)} %bitcast.118) | data formatting | bytes 8388608 | tf_op jit(solution)/shard_map/while/body/eval_jaxpr/gather | solution.py:77
  402.3 4.5 fusion.80
  411.9 3.9 fusion.89
  422.4 4.4 fusion.90
  429.3 4.0 constant_dynamic-slice_fusion.9
  440.6 4.9 gather_fusion
  445.5 7.5 %copy.113 = bf16[4,8,2,128,256]{3,1,4,0,2:T(8,128)(2,1)} copy(bf16[4,8,2,128,256]{4,3,2,1,0:T(8,128)(2,1)} %bitcast.118) | data formatting | bytes 8388608 | tf_op jit(solution)/shard_map/while/body/eval_jaxpr/gather | solution.py:77
  453.0 4.5 fusion.80
  462.5 3.9 fusion.89
  473.1 4.4 fusion.90
  480.0 4.1 constant_dynamic-slice_fusion.9
  491.3 4.9 gather_fusion
  496.2 7.5 %copy.113 = bf16[4,8,2,128,256]{3,1,4,0,2:T(8,128)(2,1)} copy(bf16[4,8,2,128,256]{4,3,2,1,0:T(8,128)(2,1)} %bitcast.118) | data formatting | bytes 8388608 | tf_op jit(solution)/shard_map/while/body/eval_jaxpr/gather | solution.py:77
  503.7 4.5 fusion.80
  513.3 3.9 fusion.89
  523.8 4.4 fusion.90
  530.7 4.1 constant_dynamic-slice_fusion.9
  542.0 4.9 gather_fusion
  547.0 7.5 %copy.113 = bf16[4,8,2,128,256]{3,1,4,0,2:T(8,128)(2,1)} copy(bf16[4,8,2,128,256]{4,3,2,1,0:T(8,128)(2,1)} %bitcast.118) | data formatting | bytes 8388608 | tf_op jit(solution)/shard_map/while/body/eval_jaxpr/gather | solution.py:77
  554.5 4.5 fusion.80
  564.0 3.9 fusion.89
  574.5 4.4 fusion.90
  581.5 4.1 constant_dynamic-slice_fusion.9
  592.8 4.9 gather_fusion
  597.7 7.5 %copy.113 = bf16[4,8,2,128,256]{3,1,4,0,2:T(8,128)(2,1)} copy(bf16[4,8,2,128,256]{4,3,2,1,0:T(8,128)(2,1)} %bitcast.118) | data formatting | bytes 8388608 | tf_op jit(solution)/shard_map/while/body/eval_jaxpr/gather | solution.py:77
  605.3 4.5 fusion.80
  614.8 3.9 fusion.89
  625.3 4.4 fusion.90
  629.7 3.8 copy.66
  636.0 30.1 %all_to_all.35 = bf16[8,512,256]{2,1,0:T(8,128)(2,1)S(1)} all-to-all(bf16[8,512,256]{2,1,0:T(8,128)(2,1)} %all_to_all.28), channel_id=1, replica_groups=mesh['head'=8,'ctx'=4] {'head'}, dimensions={0} | all-to-all | bytes 4194304 | tf_op jit(solution)/shard_map/all_to_all | solution.py:101
  668.5 3.9 copy.68
  (334 shorter events, 159.8 us)
Async XLA Ops:
  6.5 217.1 %all-gather.3.cloned.1.call-start = ((), (), s32[]{:S(2)}) async-start(), calls=%async_computation.2 | async-start | bytes 5242880 | tf_op jit(solution)/shard_map/all_gather | solution.py:61
  139.9 7.1 %copy-start.4 = (s32[32,8]{0,1:T(8,128)S(1)}, s32[32,8]{0,1:T(8,128)}, u32[]{:S(2)}) copy-start(s32[32,8]{0,1:T(8,128)} %param.11) | copy-start | bytes 3076
  143.3 31.4 %collective-permute-start = (bf16[2,512,256]{2,1,0:T(8,128)(2,1)S(1)}, bf16[2,512,256]{2,1,0:T(8,128)(2,1)S(1)}, u32[]{:S(2)}, u32[]{:S(2)}) collective-permute-start(bf16[2,512,256]{2,1,0:T(8,128)(2,1)S(1)} %slice.96), channel_id=1, source_target_pairs={{0,1},{1,2},{2,3},{4,5},{5,6},{6,7},{8,9},{9,10},{10,11},{12,13},{... | collective-permute-start | bytes 1572872 | tf_op jit(solution)/shard_map/ppermute | solution.py:16
  179.4 44.2 %copy-start.5 = (s32[2]{0:T(128)S(1)}, s32[2]{0:T(128)}, u32[]{:S(2)}) copy-start(s32[2]{0:T(128)} %param.10) | copy-start | bytes 28
  233.0 4.5 copy-start.1
  257.3 2.2 copy-start
  257.3 2.2 copy-start.3
  267.5 2.6 copy-start.2
  283.8 4.5 copy-start.1
  308.2 2.2 copy-start
  308.2 2.2 copy-start.3
  318.3 2.6 copy-start.2
  334.5 4.5 copy-start.1
  358.9 2.2 copy-start
  358.9 2.2 copy-start.3
  369.1 2.6 copy-start.2
  385.2 4.5 copy-start.1
  409.6 2.2 copy-start
  409.6 2.2 copy-start.3
  419.8 2.6 copy-start.2
  435.9 4.5 copy-start.1
  460.3 2.2 copy-start
  460.3 2.2 copy-start.3
  470.5 2.6 copy-start.2
  486.6 4.5 copy-start.1
  511.0 2.2 copy-start
  511.0 2.2 copy-start.3
  521.2 2.6 copy-start.2
  537.4 4.5 copy-start.1
  561.8 2.2 copy-start
  561.8 2.2 copy-start.3
  572.0 2.6 copy-start.2
  588.2 4.5 copy-start.1
  612.5 2.2 copy-start
  612.6 2.2 copy-start.3
  622.7 2.6 copy-start.2
Sparse Core Ops, SparseCore 0:
  142.3 81.2 all-gather.2
where the time goes:
time: 687 us; the launch traced here: 679 us
  local copies, waits for them, and re-layouts  330 us (48%)
  blocking collectives  128 us (19%)
  matrix products  66 us (10%)
  waiting for transfers between devices  60.1 us (9%)
  other arithmetic  56.3 us (8%)
  loops' own time  22 us (3%)
  between operations  13.4 us (2%)
    gather x16, local copies, waits for them, and re-layouts, attend_group(): gathered[:, jnp.maximum(listed, 0) // STRIDE]  99.7 us
    all_to_all x1, blocking collectives, local(): lax.all_to_all(jnp.stack([queries, key_rows, value_rows]), 'head', split_...  97.8 us
    squeeze x16, local copies, waits for them, and re-layouts, attend_group(): every_value_row = jnp.concatenate([window[1], picked[1]], axis=1)  42.9 us
    all_gather x1, waiting for transfers between devices, local(): gathered = lax.all_gather(candidates, 'ctx', axis=1, tiled=True)  36.5 us
    slice x8, local copies, waits for them, and re-layouts, attend_group(): picked[0]  35.7 us
    dot_general x8, matrix products, attend_group(): jnp.einsum('bhqk,bkhd->bhqd', weights_raw.astype(jnp.bfloat16), every_val...  35 us
    slice x8, local copies, waits for them, and re-layouts, band_window(): window_rows[:, offset:offset + group_size]  32.8 us
    dot_general x16, matrix products, scores_of(): jnp.einsum('bqhd,bkhd->bhqk', query_group, key_group, preferred_element_t...  31.1 us
  transfers between devices with their start and end apart: 2, of which 2 were waited for; matrix products, arithmetic and copies ran while one was open for 3% of the time, Pallas kernels for 0%

commit v1 on v0

v1 whole, which is shorter than its diff:
```python
import functools
import math

import jax
import jax.numpy as jnp
from jax import lax
from jax.experimental import pallas as pl
from jax.experimental.pallas import tpu as pltpu
from jax.sharding import PartitionSpec as P

D = 128
BLOCK = 128
BAND = 4
G = 8
NEG = -1e30
SCALE2 = D ** (-0.5) * math.log2(math.e)


def kernel(
    heads, ctxs, rows, feat,
    band_ref, list_ref, q_hbm, k_hbm, v_hbm, out_ref,
    q, k, v, kc, vc, o,
    send, recv, chain_send, chain_recv, rim_send, rim_recv, fill_sem,
):
    me = lax.axis_index("head")
    z = lax.axis_index("ctx")
    per = rows // BLOCK
    rim = BAND * BLOCK
    length = heads * rows
    rest = rows - BLOCK
    hpd = feat // D

    barrier = pltpu.get_barrier_semaphore()

    @pl.loop(1, heads)
    def _(delta):
        pl.semaphore_signal(barrier, inc=1, device_id={"head": (me + delta) % heads})

    pl.semaphore_signal(barrier, inc=1, device_id={"ctx": (z + 1) % ctxs})
    pl.semaphore_signal(barrier, inc=1, device_id={"ctx": (z + ctxs - 1) % ctxs})
    pl.semaphore_wait(barrier, heads + 1)

    def col(p):
        return pl.ds(pl.multiple_of(p * feat, 128), feat)

    def row(s, first, n):
        return pl.ds(pl.multiple_of(first + s * rows, 128), n)

    def src(kind, p):
        if kind == 0:
            return k_hbm.at[pl.ds(rest, BLOCK), col(p)]
        if kind == 1:
            return v_hbm.at[pl.ds(rest, BLOCK), col(p)]
        if kind == 2:
            return k_hbm.at[pl.ds(0, rest), col(p)]
        if kind == 3:
            return v_hbm.at[pl.ds(0, rest), col(p)]
        return q_hbm.at[:, col(p)]

    def dst(kind, s):
        if kind == 0:
            return kc.at[z * heads + s]
        if kind == 1:
            return vc.at[z * heads + s]
        if kind == 2:
            return k.at[row(s, rim, rest), :]
        if kind == 3:
            return v.at[row(s, rim, rest), :]
        return q.at[row(s, 0, rows), :]

    def outgoing(kind, delta):
        return pltpu.make_async_remote_copy(
            src_ref=src(kind, (me + delta) % heads),
            dst_ref=dst(kind, me),
            send_sem=send.at[kind, delta],
            recv_sem=recv.at[kind, delta],
            device_id={"head": (me + delta) % heads},
        )

    def incoming(kind, delta):
        s = (me + heads - delta) % heads
        return pltpu.make_async_remote_copy(
            src_ref=src(kind, s),
            dst_ref=dst(kind, s),
            send_sem=send.at[kind, delta],
            recv_sem=recv.at[kind, delta],
            device_id={"head": s},
        )

    def own(kind):
        return pltpu.make_async_copy(src(kind, me), dst(kind, me), send.at[kind, 0])

    def start(kind):
        @pl.loop(1, heads)
        def _(delta):
            outgoing(kind, delta).start()

        own(kind).start()

    def arrive(kind):
        @pl.loop(1, heads)
        def _(delta):
            incoming(kind, delta).wait_recv()

        own(kind).wait()

    def sent(kind):
        @pl.loop(1, heads)
        def _(delta):
            outgoing(kind, delta).wait_send()

    def fill(which, s):
        big, cand = (k, kc) if which == 0 else (v, vc)
        return pltpu.make_async_copy(
            cand.at[z * heads + s], big.at[row(s, rim + rest, BLOCK), :], fill_sem.at[which, s]
        )

    def chain(which, t, group):
        buf = kc if which == 0 else vc
        part = buf.at[pl.ds(group * heads, heads)]
        return pltpu.make_async_remote_copy(
            src_ref=part,
            dst_ref=part,
            send_sem=chain_send.at[which, t],
            recv_sem=chain_recv.at[which, t],
            device_id={"ctx": (z + 1) % ctxs},
        )

    def edge(which):
        big = k if which == 0 else v
        return pltpu.make_async_remote_copy(
            src_ref=big.at[pl.ds(length, rim), :],
            dst_ref=big.at[pl.ds(0, rim), :],
            send_sem=rim_send.at[which],
            recv_sem=rim_recv.at[which],
            device_id={"ctx": (z + 1) % ctxs},
        )

    start(0)
    start(1)
    if rest:
        start(2)

    @pl.when(z == 0)
    def _():
        k[pl.ds(0, rim), :] = jnp.zeros((rim, feat), k.dtype)
        v[pl.ds(0, rim), :] = jnp.zeros((rim, feat), v.dtype)

    arrive(0)
    arrive(1)

    @pl.when(z + 1 < ctxs)
    def _():
        chain(0, 0, z).start()
        chain(1, 0, z).start()

    @pl.loop(0, heads)
    def _(s):
        fill(0, s).start()
        fill(1, s).start()

    if rest:
        start(3)
    start(4)

    @pl.loop(0, heads)
    def _(s):
        fill(0, s).wait()
        fill(1, s).wait()

    if rest:
        arrive(2)
        arrive(3)

    @pl.when(z + 1 < ctxs)
    def _():
        edge(0).start()
        edge(1).start()

    @pl.loop(0, ctxs - 1)
    def _(t):
        @pl.when((t > 0) & (z + 1 < ctxs) & (z >= t))
        def _():
            chain(0, t, z - t).start()
            chain(1, t, z - t).start()

        @pl.when(z >= t + 1)
        def _():
            chain(0, t, z - 1 - t).wait_recv()
            chain(1, t, z - 1 - t).wait_recv()

    @pl.when(z > 0)
    def _():
        edge(0).wait_recv()
        edge(1).wait_recv()

    arrive(4)

    tri = lax.broadcasted_iota(jnp.int32, (BLOCK, BLOCK), 1) <= lax.broadcasted_iota(
        jnp.int32, (BLOCK, BLOCK), 0
    )
    first = z * (length // BLOCK)

    def attend(b, h):
        hs = pl.ds(h * D, D)
        base = pl.multiple_of(b * BLOCK, 128)
        qb = q[pl.ds(base, BLOCK), hs]
        window = pl.ds(base, (BAND + 1) * BLOCK)
        listed = [list_ref[b, g] for g in range(G)]
        slots = [jnp.maximum(j, 0) // per for j in listed]
        keys = jnp.concatenate([k[window, hs]] + [kc[i, :, hs] for i in slots], axis=0)
        values = jnp.concatenate([v[window, hs]] + [vc[i, :, hs] for i in slots], axis=0)
        s = lax.dot_general(
            qb, keys, (((1,), (1,)), ((), ())), preferred_element_type=jnp.float32
        )
        parts = [s[:, i * BLOCK : (i + 1) * BLOCK] for i in range(BAND + 1 + G)]
        parts[BAND] = jnp.where(tri, parts[BAND], NEG)
        reach = band_ref[h]
        bias = [
            jnp.where((reach >= BAND - i) & (first + b >= BAND - i), 0.0, NEG) for i in range(BAND)
        ]
        bias = bias + [None] + [jnp.where(j >= 0, 0.0, NEG) for j in listed]
        top = parts[BAND]
        for part, off in zip(parts, bias):
            if off is not None:
                top = jnp.maximum(top, part + off)
        top = jnp.max(top, axis=1, keepdims=True) * SCALE2
        weights = []
        for part, off in zip(parts, bias):
            shift = top if off is None else top - off
            weights.append(jnp.exp2(part * SCALE2 - shift))
        total = functools.reduce(jnp.add, weights)
        total = jnp.sum(total, axis=1, keepdims=True)
        w = jnp.concatenate([x.astype(jnp.bfloat16) for x in weights], axis=1)
        acc = jnp.dot(w, values, preferred_element_type=jnp.float32)
        o[pl.ds(base, BLOCK), hs] = (acc / total).astype(o.dtype)

    def give(delta):
        p = (me + delta) % heads
        return pltpu.make_async_remote_copy(
            src_ref=o.at[row(p, 0, rows), :],
            dst_ref=out_ref.at[:, col(me)],
            send_sem=send.at[5, delta],
            recv_sem=recv.at[5, delta],
            device_id={"head": p},
        )

    def take(delta):
        p = (me + heads - delta) % heads
        return pltpu.make_async_remote_copy(
            src_ref=o.at[row(p, 0, rows), :],
            dst_ref=out_ref.at[:, col(p)],
            send_sem=send.at[5, delta],
            recv_sem=recv.at[5, delta],
            device_id={"head": p},
        )

    def group(delta):
        @pl.loop(0, per)
        def _(j):
            for h in range(hpd):
                attend((me + delta) % heads * per + j, h)

    @pl.loop(1, heads)
    def _(delta):
        group(delta)
        give(delta).start()

    group(0)
    mine = pltpu.make_async_copy(o.at[row(me, 0, rows), :], out_ref.at[:, col(me)], send.at[5, 0])
    mine.start()

    for kind in range(5):
        if rest or kind not in (2, 3):
            sent(kind)

    @pl.when(z + 1 < ctxs)
    def _():
        edge(0).wait_send()
        edge(1).wait_send()

    @pl.loop(0, ctxs - 1)
    def _(t):
        @pl.when((z + 1 < ctxs) & (z >= t))
        def _():
            chain(0, t, z - t).wait_send()
            chain(1, t, z - t).wait_send()

    @pl.loop(1, heads)
    def _(delta):
        give(delta).wait_send()
        take(delta).wait_recv()

    mine.wait()


def solution(mesh):
    heads, ctxs = mesh.shape["head"], mesh.shape["ctx"]

    def local(queries, key_rows, value_rows, band_blocks, global_list):
        rows, width = queries.shape
        feat = width // heads
        length = rows * heads
        rim = BAND * BLOCK
        assert rows % BLOCK == 0 and BAND % (rows // BLOCK) == 0
        bf = jnp.bfloat16
        dma = pltpu.SemaphoreType.DMA
        return pl.pallas_call(
            functools.partial(kernel, heads, ctxs, rows, feat),
            out_shape=jax.ShapeDtypeStruct((rows, width), bf),
            in_specs=[pl.BlockSpec(memory_space=pltpu.SMEM)] * 2
            + [pl.BlockSpec(memory_space=pl.ANY)] * 3,
            out_specs=pl.BlockSpec(memory_space=pl.ANY),
            scratch_shapes=[
                pltpu.VMEM((length, feat), bf),
                pltpu.VMEM((length + rim, feat), bf),
                pltpu.VMEM((length + rim, feat), bf),
                pltpu.VMEM((ctxs * heads, BLOCK, feat), bf),
                pltpu.VMEM((ctxs * heads, BLOCK, feat), bf),
                pltpu.VMEM((length, feat), bf),
                dma((6, heads)),
                dma((6, heads)),
                dma((2, ctxs)),
                dma((2, ctxs)),
                dma((2,)),
                dma((2,)),
                dma((2, heads)),
            ],
            compiler_params=pltpu.CompilerParams(
                collective_id=0, has_side_effects=True, vmem_limit_bytes=48 * 1024 * 1024
            ),
        )(band_blocks, global_list, queries, key_rows, value_rows)

    in_specs = (
        P(("ctx", "head"), None),
        P(("ctx", "head"), None),
        P(("ctx", "head"), None),
        P("head"),
        P("ctx", None),
    )
    return jax.shard_map(
        local, mesh=mesh, in_specs=in_specs, out_specs=P(("ctx", "head"), None), check_vma=False
    )
```

time: 687 us -> 151 us (0.22)
  the two profiles are of different devices: /device:TPU:16 before, /device:TPU:27 now
where the time goes in v1:
time: 151 us
  Pallas kernels  147 us (97%)
  local copies, waits for them, and re-layouts  4.33 us (3%)
    pallas_call x1, Pallas kernels, local(): pl.pallas_call(functools.partial(kernel, heads, ctxs, rows, feat), out_sh...  147 us
    unnamed x6, local copies, waits for them, and re-layouts  4.33 us

profile of v1, /device:TPU:27, one launch (start us, length us, event | category | flops | bytes accessed | tf_op | source)
XLA Modules:
  0.0 151.1 jit_solution(7058099928228823731)
XLA Ops:
  0.0 0.8 copy.6.list_ref
  0.8 0.0 copy-start
  0.8 1.6 %copy-done = bf16[512,2048]{1,0:T(8,128)(2,1)S(1)} copy-done((bf16[512,2048]{1,0:T(8,128)(2,1)S(1)}, bf16[512,2048]{1,0:T(8,128)(2,1)}, u32[]{:S(2)}) %copy-start) | copy-done | bytes 2097176
  2.4 0.0 copy-start.1
  2.4 0.7 copy-done.1
  3.0 146.8 %shard_map.55 = bf16[512,2048]{1,0:T(8,128)(2,1)S(1)} custom-call(s32[2]{0:T(128)S(1)} %copy-done.1, s32[32,8]{1,0:T(8,128)S(1)} %copy.6.list_ref, bf16[512,2048]{1,0:T(8,128)(2,1)S(1)} %copy-done, bf16[512,2048]{1,0:T(8,128)(2,1)} %k_hbm.1, bf16[512,2048]{1,0:T(8,128)(2,1)} %v_hbm.1), custom_call_target="tpu_custom_call" | custom-call | tf_op jit(solution)/shard_map/pallas_call | solution.py:308
  149.8 1.3 copy.8
Async XLA Ops:
  0.8 1.6 %copy-start = (bf16[512,2048]{1,0:T(8,128)(2,1)S(1)}, bf16[512,2048]{1,0:T(8,128)(2,1)}, u32[]{:S(2)}) copy-start(bf16[512,2048]{1,0:T(8,128)(2,1)} %q_hbm.1) | copy-start | bytes 6291460
  2.4 0.7 copy-start.1

commit v2 on v1

v2 whole, which is shorter than its diff:
```python
import functools
import math

import jax
import jax.numpy as jnp
from jax import lax
from jax.experimental import pallas as pl
from jax.experimental.pallas import tpu as pltpu
from jax.sharding import PartitionSpec as P

D = 128
BLOCK = 128
BAND = 4
G = 8
NEG = -1e30
SCALE2 = D ** (-0.5) * math.log2(math.e)


def kernel(
    heads, ctxs, rows, feat,
    band_ref, list_ref, q_hbm, k_hbm, v_hbm, out_ref,
    q, k, v, kc, vc, o, acc, top, total,
    send, recv, give_send, give_recv, chain_send, chain_recv, rim_send, rim_recv, fill_sem,
):
    me = lax.axis_index("head")
    z = lax.axis_index("ctx")
    per = rows // BLOCK
    rim = BAND * BLOCK
    length = heads * rows
    rest = rows - BLOCK
    hpd = feat // D

    barrier = pltpu.get_barrier_semaphore()

    @pl.loop(1, heads)
    def _(delta):
        pl.semaphore_signal(barrier, inc=1, device_id={"head": (me + delta) % heads})

    pl.semaphore_signal(barrier, inc=1, device_id={"ctx": (z + 1) % ctxs})
    pl.semaphore_signal(barrier, inc=1, device_id={"ctx": (z + ctxs - 1) % ctxs})
    pl.semaphore_wait(barrier, heads + 1)

    def col(p):
        return pl.ds(pl.multiple_of(p * feat, 128), feat)

    def row(s, first, n):
        return pl.ds(pl.multiple_of(first + s * rows, 128), n)

    k_rest, v_rest, q_all = 2 * hpd, 2 * hpd + 1, 2 * hpd + 2

    def last(which, h):
        return 2 * h + which

    def src(kind, p):
        if kind < k_rest:
            hbm = v_hbm if kind % 2 else k_hbm
            at = pl.multiple_of(p * feat + kind // 2 * D, 128)
            return hbm.at[pl.ds(rest, BLOCK), pl.ds(at, D)]
        if kind == k_rest:
            return k_hbm.at[pl.ds(0, rest), col(p)]
        if kind == v_rest:
            return v_hbm.at[pl.ds(0, rest), col(p)]
        return q_hbm.at[:, col(p)]

    def dst(kind, s):
        if kind < k_rest:
            return (vc if kind % 2 else kc)[kind // 2].at[z * heads + s]
        if kind == k_rest:
            return k.at[row(s, rim, rest), :]
        if kind == v_rest:
            return v.at[row(s, rim, rest), :]
        return q.at[row(s, 0, rows), :]

    def outgoing(kind, delta):
        return pltpu.make_async_remote_copy(
            src_ref=src(kind, (me + delta) % heads),
            dst_ref=dst(kind, me),
            send_sem=send.at[kind, delta],
            recv_sem=recv.at[kind, delta],
            device_id={"head": (me + delta) % heads},
        )

    def incoming(kind, delta):
        s = (me + heads - delta) % heads
        return pltpu.make_async_remote_copy(
            src_ref=src(kind, s),
            dst_ref=dst(kind, s),
            send_sem=send.at[kind, delta],
            recv_sem=recv.at[kind, delta],
            device_id={"head": s},
        )

    def own(kind):
        return pltpu.make_async_copy(src(kind, me), dst(kind, me), send.at[kind, 0])

    def start(kind):
        @pl.loop(1, heads)
        def _(delta):
            outgoing(kind, delta).start()

        own(kind).start()

    def arrive(kind):
        @pl.loop(1, heads)
        def _(delta):
            incoming(kind, delta).wait_recv()

        own(kind).wait()

    def sent(kind):
        @pl.loop(1, heads)
        def _(delta):
            outgoing(kind, delta).wait_send()

    def fill(which, s, h):
        big, cand = (k, kc) if which == 0 else (v, vc)
        return pltpu.make_async_copy(
            cand[h].at[z * heads + s],
            big.at[row(s, rim + rest, BLOCK), pl.ds(h * D, D)],
            fill_sem.at[which, s, h],
        )

    def chain(which, t, group, s, h):
        part = (kc if which == 0 else vc)[h].at[group * heads + s]
        return pltpu.make_async_remote_copy(
            src_ref=part,
            dst_ref=part,
            send_sem=chain_send.at[which, t, s, h],
            recv_sem=chain_recv.at[which, t, s, h],
            device_id={"ctx": (z + 1) % ctxs},
        )

    def edge(which):
        big = k if which == 0 else v
        return pltpu.make_async_remote_copy(
            src_ref=big.at[pl.ds(length, rim), :],
            dst_ref=big.at[pl.ds(0, rim), :],
            send_sem=rim_send.at[which],
            recv_sem=rim_recv.at[which],
            device_id={"ctx": (z + 1) % ctxs},
        )

    for kind in range(k_rest):
        start(kind)
    if rest:
        start(k_rest)

    @pl.when(z == 0)
    def _():
        k[pl.ds(0, rim), :] = jnp.zeros((rim, feat), k.dtype)
        v[pl.ds(0, rim), :] = jnp.zeros((rim, feat), v.dtype)

    if rest:
        start(v_rest)
    start(q_all)

    def pass_on(s, h):
        @pl.when(z + 1 < ctxs)
        def _():
            chain(0, 0, z, s, h).start()
            chain(1, 0, z, s, h).start()

        fill(0, s, h).start()
        fill(1, s, h).start()

    def forward(t, s, h):
        for which in range(2):
            chain(which, t - 1, z - t, s, h).wait_recv()
            chain(which, t, z - t, s, h).start()

    def forward_all(t, h):
        @pl.when((z + 1 < ctxs) & (z >= t))
        def _():
            @pl.loop(0, heads)
            def _(delta):
                forward(t, (me + heads - delta) % heads, h)

    for h in range(hpd):
        own(last(0, h)).wait()
        own(last(1, h)).wait()
        pass_on(me, h)

        @pl.loop(1, heads)
        def _(delta):
            incoming(last(0, h), delta).wait_recv()
            incoming(last(1, h), delta).wait_recv()
            pass_on((me + heads - delta) % heads, h)

        if h == 0:

            @pl.loop(1, ctxs - 1)
            def _(t):
                forward_all(t, 0)

    @pl.loop(0, heads)
    def _(s):
        for h in range(hpd):
            fill(0, s, h).wait()
            fill(1, s, h).wait()

    if rest:
        arrive(k_rest)
        arrive(v_rest)

    @pl.when(z + 1 < ctxs)
    def _():
        edge(0).start()
        edge(1).start()

    for h in range(1, hpd):
        forward_all(1, h)

    tri = lax.broadcasted_iota(jnp.int32, (BLOCK, BLOCK), 1) <= lax.broadcasted_iota(
        jnp.int32, (BLOCK, BLOCK), 0
    )
    first = z * (length // BLOCK)

    def weigh(parts, bias, peak):
        weights = []
        for part, off in zip(parts, bias):
            shift = peak if off is None else peak - off
            weights.append(jnp.exp2(part * SCALE2 - shift))
        added = jnp.sum(functools.reduce(jnp.add, weights), axis=1, keepdims=True)
        return jnp.concatenate([x.astype(jnp.bfloat16) for x in weights], axis=1), added

    def scores(qb, keys):
        s = lax.dot_general(
            qb, keys, (((1,), (1,)), ((), ())), preferred_element_type=jnp.float32
        )
        return [s[:, i : i + BLOCK] for i in range(0, s.shape[1], BLOCK)]

    def place(b, h):
        return pl.ds(pl.multiple_of(b * BLOCK, 128), BLOCK), pl.ds(h * D, D)

    def near(b, h):
        at = place(b, h)
        window = pl.ds(pl.multiple_of(b * BLOCK, 128), (BAND + 1) * BLOCK)
        parts = scores(q[at], k[window, at[1]])
        parts[BAND] = jnp.where(tri, parts[BAND], NEG)
        reach = band_ref[h]
        bias = [
            jnp.where((reach >= BAND - i) & (first + b >= BAND - i), 0.0, NEG) for i in range(BAND)
        ]
        peak = parts[BAND]
        for part, off in zip(parts, bias):
            peak = jnp.maximum(peak, part + off)
        peak = jnp.max(peak, axis=1, keepdims=True) * SCALE2
        w, added = weigh(parts, bias + [None], peak)
        acc[at] = jnp.dot(w, v[window, at[1]], preferred_element_type=jnp.float32)
        top[at] = jnp.broadcast_to(peak, (BLOCK, D))
        total[at] = jnp.broadcast_to(added, (BLOCK, D))

    def far(b, h):
        at = place(b, h)
        listed = [list_ref[b, g] for g in range(G)]
        slots = [jnp.maximum(j, 0) // per for j in listed]
        keys = jnp.concatenate([kc[h][i] for i in slots], axis=0)
        values = jnp.concatenate([vc[h][i] for i in slots], axis=0)
        parts = scores(q[at], keys)
        bias = [jnp.where(j >= 0, 0.0, NEG) for j in listed]
        peak = functools.reduce(jnp.maximum, [part + off for part, off in zip(parts, bias)])
        before = top[at]
        peak = jnp.maximum(before, jnp.max(peak, axis=1, keepdims=True) * SCALE2)
        w, added = weigh(parts, bias, peak)
        keep = jnp.exp2(before - peak)
        blend = acc[at] * keep + jnp.dot(w, values, preferred_element_type=jnp.float32)
        o[at] = (blend / (total[at] * keep + added)).astype(o.dtype)

    def give(delta, h):
        p = (me + delta) % heads
        return pltpu.make_async_remote_copy(
            src_ref=o.at[row(p, 0, rows), pl.ds(h * D, D)],
            dst_ref=out_ref.at[:, pl.ds(pl.multiple_of(me * feat + h * D, 128), D)],
            send_sem=give_send.at[h, delta],
            recv_sem=give_recv.at[h, delta],
            device_id={"head": p},
        )

    def take(delta, h):
        p = (me + heads - delta) % heads
        return pltpu.make_async_remote_copy(
            src_ref=o.at[row(p, 0, rows), pl.ds(h * D, D)],
            dst_ref=out_ref.at[:, pl.ds(pl.multiple_of(p * feat + h * D, 128), D)],
            send_sem=give_send.at[h, delta],
            recv_sem=give_recv.at[h, delta],
            device_id={"head": p},
        )

    def mine(h):
        return pltpu.make_async_copy(
            o.at[row(me, 0, rows), pl.ds(h * D, D)],
            out_ref.at[:, pl.ds(pl.multiple_of(me * feat + h * D, 128), D)],
            give_send.at[h, 0],
        )

    def near_group(s):
        @pl.loop(0, per)
        def _(j):
            for h in range(hpd):
                near(s * per + j, h)

    def finish(s, delta, h):
        pair = math.gcd(per, 2)

        @pl.loop(0, per // pair)
        def _(j):
            for i in range(pair):
                far(s * per + j * pair + i, h)

        @pl.when(delta == 0)
        def _():
            mine(h).start()

        @pl.when(delta > 0)
        def _():
            give(delta, h).start()

    inner = rim // rows

    @pl.loop(0, heads)
    def _(delta):
        s = (me + heads - delta) % heads

        @pl.when(delta == 0)
        def _():
            own(q_all).wait()

        @pl.when(delta > 0)
        def _():
            incoming(q_all, delta).wait_recv()

        @pl.when(s >= inner)
        def _():
            near_group(s)

        for h in range(1, hpd):

            @pl.loop(2, ctxs - 1)
            def _(t):
                @pl.when((z + 1 < ctxs) & (z >= t))
                def _():
                    forward(t, s, h)

    for h in range(hpd):

        @pl.when(z + 1 == ctxs)
        def _():
            @pl.loop(0, ctxs - 1)
            def _(t):
                @pl.loop(0, heads)
                def _(s):
                    chain(0, t, z - 1 - t, s, h).wait_recv()
                    chain(1, t, z - 1 - t, s, h).wait_recv()

        if h == 0:

            @pl.loop(1, heads + 1)
            def _(step):
                delta = step % heads
                s = (me + delta) % heads

                @pl.when(s >= inner)
                def _():
                    finish(s, delta, h)

            @pl.when(z > 0)
            def _():
                edge(0).wait_recv()
                edge(1).wait_recv()

            @pl.loop(0, inner)
            def _(s):
                near_group(s)
                finish(s, (s + heads - me) % heads, h)
        else:

            @pl.loop(1, heads + 1)
            def _(step):
                delta = step % heads
                finish((me + delta) % heads, delta, h)

    for kind in range(q_all + 1):
        if rest or kind not in (k_rest, v_rest):
            sent(kind)

    @pl.when(z + 1 < ctxs)
    def _():
        edge(0).wait_send()
        edge(1).wait_send()

    @pl.loop(0, ctxs - 1)
    def _(t):
        @pl.when((z + 1 < ctxs) & (z >= t))
        def _():
            @pl.loop(0, heads)
            def _(s):
                for h in range(hpd):
                    chain(0, t, z - t, s, h).wait_send()
                    chain(1, t, z - t, s, h).wait_send()

    @pl.loop(1, heads)
    def _(delta):
        for h in range(hpd):
            give(delta, h).wait_send()
            take(delta, h).wait_recv()

    for h in range(hpd):
        mine(h).wait()


def solution(mesh):
    heads, ctxs = mesh.shape["head"], mesh.shape["ctx"]

    def local(queries, key_rows, value_rows, band_blocks, global_list):
        rows, width = queries.shape
        feat = width // heads
        length = rows * heads
        rim = BAND * BLOCK
        assert rows % BLOCK == 0 and BAND % (rows // BLOCK) == 0
        bf = jnp.bfloat16
        dma = pltpu.SemaphoreType.DMA
        return pl.pallas_call(
            functools.partial(kernel, heads, ctxs, rows, feat),
            out_shape=jax.ShapeDtypeStruct((rows, width), bf),
            in_specs=[pl.BlockSpec(memory_space=pltpu.SMEM)] * 2
            + [pl.BlockSpec(memory_space=pl.ANY)] * 3,
            out_specs=pl.BlockSpec(memory_space=pl.ANY),
            scratch_shapes=[
                pltpu.VMEM((length, feat), bf),
                pltpu.VMEM((length + rim, feat), bf),
                pltpu.VMEM((length + rim, feat), bf),
                [pltpu.VMEM((ctxs * heads, BLOCK, D), bf) for _ in range(feat // D)],
                [pltpu.VMEM((ctxs * heads, BLOCK, D), bf) for _ in range(feat // D)],
                pltpu.VMEM((length, feat), bf),
                pltpu.VMEM((length, feat), jnp.float32),
                pltpu.VMEM((length, feat), jnp.float32),
                pltpu.VMEM((length, feat), jnp.float32),
                dma((2 * (feat // D) + 3, heads)),
                dma((2 * (feat // D) + 3, heads)),
                dma((feat // D, heads)),
                dma((feat // D, heads)),
                dma((2, ctxs, heads, feat // D)),
                dma((2, ctxs, heads, feat // D)),
                dma((2,)),
                dma((2,)),
                dma((2, heads, feat // D)),
            ],
            compiler_params=pltpu.CompilerParams(
                collective_id=0, has_side_effects=True, vmem_limit_bytes=48 * 1024 * 1024
            ),
        )(band_blocks, global_list, queries, key_rows, value_rows)

    in_specs = (
        P(("ctx", "head"), None),
        P(("ctx", "head"), None),
        P(("ctx", "head"), None),
        P("head"),
        P("ctx", None),
    )
    return jax.shard_map(
        local, mesh=mesh, in_specs=in_specs, out_specs=P(("ctx", "head"), None), check_vma=False
    )
```

time: 151 us -> 129 us (0.85)
  the two profiles are of different devices: /device:TPU:27 before, /device:TPU:0 now
where the time goes in v2:
time: 129 us
  Pallas kernels  124 us (96%)
  local copies, waits for them, and re-layouts  4.33 us (3%)
    pallas_call x1, Pallas kernels, local(): pl.pallas_call(functools.partial(kernel, heads, ctxs, rows, feat), out_sh...  124 us
    unnamed x6, local copies, waits for them, and re-layouts  4.33 us

profile of v2, /device:TPU:0, one launch (start us, length us, event | category | flops | bytes accessed | tf_op | source)
XLA Modules:
  0.0 128.7 jit_solution(7715842964663451604)
XLA Ops:
  0.0 0.8 copy.6.list_ref
  0.8 0.0 copy-start
  0.8 1.6 %copy-done = bf16[512,2048]{1,0:T(8,128)(2,1)S(1)} copy-done((bf16[512,2048]{1,0:T(8,128)(2,1)S(1)}, bf16[512,2048]{1,0:T(8,128)(2,1)}, u32[]{:S(2)}) %copy-start) | copy-done | bytes 2097176
  2.4 0.0 copy-start.1
  2.4 0.7 copy-done.1
  3.0 124.4 %shard_map.55 = bf16[512,2048]{1,0:T(8,128)(2,1)S(1)} custom-call(s32[2]{0:T(128)S(1)} %copy-done.1, s32[32,8]{1,0:T(8,128)S(1)} %copy.6.list_ref, bf16[512,2048]{1,0:T(8,128)(2,1)S(1)} %copy-done, bf16[512,2048]{1,0:T(8,128)(2,1)} %k_hbm.1, bf16[512,2048]{1,0:T(8,128)(2,1)} %v_hbm.1), custom_call_target="tpu_custom_call" | custom-call | tf_op jit(solution)/shard_map/pallas_call | solution.py:422
  127.4 1.3 %copy.8 = bf16[512,2048]{1,0:T(8,128)(2,1)} copy(bf16[512,2048]{1,0:T(8,128)(2,1)S(1)} %shard_map.55) | data formatting | bytes 4194304
Async XLA Ops:
  0.8 1.6 %copy-start = (bf16[512,2048]{1,0:T(8,128)(2,1)S(1)}, bf16[512,2048]{1,0:T(8,128)(2,1)}, u32[]{:S(2)}) copy-start(bf16[512,2048]{1,0:T(8,128)(2,1)} %q_hbm.1) | copy-start | bytes 6291460
  2.4 0.7 copy-start.1

commit v3 on v2

--- a/solution.py
+++ b/solution.py
@@ -46,30 +46,31 @@
     def row(s, first, n):
         return pl.ds(pl.multiple_of(first + s * rows, 128), n)
 
-    k_rest, v_rest, q_all = 2 * hpd, 2 * hpd + 1, 2 * hpd + 2
-
     def last(which, h):
         return 2 * h + which
 
+    def before(which, h):
+        return 2 * hpd + 2 * h + which
+
+    def query(h):
+        return 4 * hpd + h
+
+    kinds = range(5 * hpd)
+
     def src(kind, p):
-        if kind < k_rest:
-            hbm = v_hbm if kind % 2 else k_hbm
-            at = pl.multiple_of(p * feat + kind // 2 * D, 128)
-            return hbm.at[pl.ds(rest, BLOCK), pl.ds(at, D)]
-        if kind == k_rest:
-            return k_hbm.at[pl.ds(0, rest), col(p)]
-        if kind == v_rest:
-            return v_hbm.at[pl.ds(0, rest), col(p)]
-        return q_hbm.at[:, col(p)]
+        if kind >= 4 * hpd:
+            hbm, h, at = q_hbm, kind - 4 * hpd, pl.ds(0, rows)
+        else:
+            hbm, h = (v_hbm if kind % 2 else k_hbm), kind // 2 % hpd
+            at = pl.ds(rest, BLOCK) if kind < 2 * hpd else pl.ds(0, rest)
+        return hbm.at[at, pl.ds(pl.multiple_of(p * feat + h * D, 128), D)]
 
     def dst(kind, s):
-        if kind < k_rest:
+        if kind >= 4 * hpd:
+            return q.at[row(s, 0, rows), pl.ds((kind - 4 * hpd) * D, D)]
+        if kind < 2 * hpd:
             return (vc if kind % 2 else kc)[kind // 2].at[z * heads + s]
-        if kind == k_rest:
-            return k.at[row(s, rim, rest), :]
-        if kind == v_rest:
-            return v.at[row(s, rim, rest), :]
-        return q.at[row(s, 0, rows), :]
+        return (v if kind % 2 else k).at[row(s, rim, rest), pl.ds(kind // 2 % hpd * D, D)]
 
     def outgoing(kind, delta):
         return pltpu.make_async_remote_copy(
@@ -130,29 +131,31 @@
             device_id={"ctx": (z + 1) % ctxs},
         )
 
-    def edge(which):
+    def edge(which, h):
         big = k if which == 0 else v
-        return pltpu.make_async_remote_copy(
-            src_ref=big.at[pl.ds(length, rim), :],
-            dst_ref=big.at[pl.ds(0, rim), :],
-            send_sem=rim_send.at[which],
-            recv_sem=rim_recv.at[which],
+        hs = pl.ds(h * D, D)
+        return pltpu.make_async_remote_copy(
+            src_ref=big.at[pl.ds(length, rim), hs],
+            dst_ref=big.at[pl.ds(0, rim), hs],
+            send_sem=rim_send.at[which, h],
+            recv_sem=rim_recv.at[which, h],
             device_id={"ctx": (z + 1) % ctxs},
         )
 
-    for kind in range(k_rest):
+    def start_head(h):
+        if rest:
+            start(before(0, h))
+            start(before(1, h))
+        start(query(h))
+
+    for kind in range(2 * hpd):
         start(kind)
-    if rest:
-        start(k_rest)
+    start_head(0)
 
     @pl.when(z == 0)
     def _():
         k[pl.ds(0, rim), :] = jnp.zeros((rim, feat), k.dtype)
         v[pl.ds(0, rim), :] = jnp.zeros((rim, feat), v.dtype)
-
-    if rest:
-        start(v_rest)
-    start(q_all)
 
     def pass_on(s, h):
         @pl.when(z + 1 < ctxs)
@@ -198,15 +201,19 @@
             fill(0, s, h).wait()
             fill(1, s, h).wait()
 
-    if rest:
-        arrive(k_rest)
-        arrive(v_rest)
-
-    @pl.when(z + 1 < ctxs)
-    def _():
-        edge(0).start()
-        edge(1).start()
-
+    def keys_here(h):
+        if rest:
+            arrive(before(0, h))
+            arrive(before(1, h))
+        if h + 1 < hpd:
+            start_head(h + 1)
+
+        @pl.when(z + 1 < ctxs)
+        def _():
+            edge(0, h).start()
+            edge(1, h).start()
+
+    keys_here(0)
     for h in range(1, hpd):
         forward_all(1, h)
 
@@ -293,19 +300,16 @@
             give_send.at[h, 0],
         )
 
-    def near_group(s):
-        @pl.loop(0, per)
+    def blocks(s, part, h):
+        at_once = math.gcd(per, 4)
+
+        @pl.loop(0, per // at_once)
         def _(j):
-            for h in range(hpd):
-                near(s * per + j, h)
+            for i in range(at_once):
+                part(s * per + j * at_once + i, h)
 
     def finish(s, delta, h):
-        pair = math.gcd(per, 2)
-
-        @pl.loop(0, per // pair)
-        def _(j):
-            for i in range(pair):
-                far(s * per + j * pair + i, h)
+        blocks(s, far, h)
 
         @pl.when(delta == 0)
         def _():
@@ -317,31 +321,34 @@
 
     inner = rim // rows
 
-    @pl.loop(0, heads)
-    def _(delta):
-        s = (me + heads - delta) % heads
-
-        @pl.when(delta == 0)
-        def _():
-            own(q_all).wait()
-
-        @pl.when(delta > 0)
-        def _():
-            incoming(q_all, delta).wait_recv()
-
-        @pl.when(s >= inner)
-        def _():
-            near_group(s)
-
-        for h in range(1, hpd):
-
-            @pl.loop(2, ctxs - 1)
-            def _(t):
-                @pl.when((z + 1 < ctxs) & (z >= t))
-                def _():
-                    forward(t, s, h)
-
     for h in range(hpd):
+        if h > 0:
+            keys_here(h)
+
+        @pl.loop(0, heads)
+        def _(delta):
+            s = (me + heads - delta) % heads
+
+            @pl.when(delta == 0)
+            def _():
+                own(query(h)).wait()
+
+            @pl.when(delta > 0)
+            def _():
+                incoming(query(h), delta).wait_recv()
+
+            @pl.when(s >= inner)
+            def _():
+                blocks(s, near, h)
+
+            if h == 0:
+                for later in range(1, hpd):
+
+                    @pl.loop(2, ctxs - 1)
+                    def _(t):
+                        @pl.when((z + 1 < ctxs) & (z >= t))
+                        def _():
+                            forward(t, s, later)
 
         @pl.when(z + 1 == ctxs)
         def _():
@@ -352,41 +359,34 @@
                     chain(0, t, z - 1 - t, s, h).wait_recv()
                     chain(1, t, z - 1 - t, s, h).wait_recv()
 
-        if h == 0:
-
-            @pl.loop(1, heads + 1)
-            def _(step):
-                delta = step % heads
-                s = (me + delta) % heads
-
-                @pl.when(s >= inner)
-                def _():
-                    finish(s, delta, h)
-
-            @pl.when(z > 0)
+        @pl.loop(1, heads + 1)
+        def _(step):
+            delta = step % heads
+            s = (me + delta) % heads
+
+            @pl.when(s >= inner)
             def _():
-                edge(0).wait_recv()
-                edge(1).wait_recv()
-
-            @pl.loop(0, inner)
-            def _(s):
-                near_group(s)
-                finish(s, (s + heads - me) % heads, h)
-        else:
-
-            @pl.loop(1, heads + 1)
-            def _(step):
-                delta = step % heads
-                finish((me + delta) % heads, delta, h)
-
-    for kind in range(q_all + 1):
-        if rest or kind not in (k_rest, v_rest):
+                finish(s, delta, h)
+
+        @pl.when(z > 0)
+        def _():
+            edge(0, h).wait_recv()
+            edge(1, h).wait_recv()
+
+        @pl.loop(0, inner)
+        def _(s):
+            blocks(s, near, h)
+            finish(s, (s + heads - me) % heads, h)
+
+    for kind in kinds:
+        if rest or kind // (2 * hpd) != 1:
             sent(kind)
 
     @pl.when(z + 1 < ctxs)
     def _():
-        edge(0).wait_send()
-        edge(1).wait_send()
+        for h in range(hpd):
+            edge(0, h).wait_send()
+            edge(1, h).wait_send()
 
     @pl.loop(0, ctxs - 1)
     def _(t):
@@ -435,14 +435,14 @@
                 pltpu.VMEM((length, feat), jnp.float32),
                 pltpu.VMEM((length, feat), jnp.float32),
                 pltpu.VMEM((length, feat), jnp.float32),
-                dma((2 * (feat // D) + 3, heads)),
-                dma((2 * (feat // D) + 3, heads)),
+                dma((5 * (feat // D), heads)),
+                dma((5 * (feat // D), heads)),
                 dma((feat // D, heads)),
                 dma((feat // D, heads)),
                 dma((2, ctxs, heads, feat // D)),
                 dma((2, ctxs, heads, feat // D)),
-                dma((2,)),
-                dma((2,)),
+                dma((2, feat // D)),
+                dma((2, feat // D)),
                 dma((2, heads, feat // D)),
             ],
             compiler_params=pltpu.CompilerParams(

time: 129 us -> 114 us (0.88)
  the two profiles are of different devices: /device:TPU:0 before, /device:TPU:16 now
where the time goes in v3:
time: 114 us; the launch traced here: 113 us
  Pallas kernels  109 us (96%)
  local copies, waits for them, and re-layouts  4.33 us (4%)
    pallas_call x1, Pallas kernels, local(): pl.pallas_call(functools.partial(kernel, heads, ctxs, rows, feat), out_sh...  109 us
    unnamed x6, local copies, waits for them, and re-layouts  4.33 us

profile of v3, /device:TPU:16, one launch (start us, length us, event | category | flops | bytes accessed | tf_op | source)
XLA Modules:
  0.0 113.4 jit_solution(7928963912708396947)
XLA Ops:
  0.0 0.8 copy.6.list_ref
  0.8 0.0 copy-start
  0.8 1.6 %copy-done = bf16[512,2048]{1,0:T(8,128)(2,1)S(1)} copy-done((bf16[512,2048]{1,0:T(8,128)(2,1)S(1)}, bf16[512,2048]{1,0:T(8,128)(2,1)}, u32[]{:S(2)}) %copy-start) | copy-done | bytes 2097176
  2.4 0.0 copy-start.1
  2.4 0.7 copy-done.1
  3.0 109.1 %shard_map.55 = bf16[512,2048]{1,0:T(8,128)(2,1)S(1)} custom-call(s32[2]{0:T(128)S(1)} %copy-done.1, s32[32,8]{1,0:T(8,128)S(1)} %copy.6.list_ref, bf16[512,2048]{1,0:T(8,128)(2,1)S(1)} %copy-done, bf16[512,2048]{1,0:T(8,128)(2,1)} %k_hbm.1, bf16[512,2048]{1,0:T(8,128)(2,1)} %v_hbm.1), custom_call_target="tpu_custom_call" | custom-call | tf_op jit(solution)/shard_map/pallas_call | solution.py:422
  112.1 1.3 %copy.8 = bf16[512,2048]{1,0:T(8,128)(2,1)} copy(bf16[512,2048]{1,0:T(8,128)(2,1)S(1)} %shard_map.55) | data formatting | bytes 4194304
Async XLA Ops:
  0.8 1.6 %copy-start = (bf16[512,2048]{1,0:T(8,128)(2,1)S(1)}, bf16[512,2048]{1,0:T(8,128)(2,1)}, u32[]{:S(2)}) copy-start(bf16[512,2048]{1,0:T(8,128)(2,1)} %q_hbm.1) | copy-start | bytes 6291460
  2.4 0.7 copy-start.1

commit v4 on v3

--- a/solution.py
+++ b/solution.py
@@ -204,9 +204,10 @@
     def keys_here(h):
         if rest:
             arrive(before(0, h))
-            arrive(before(1, h))
         if h + 1 < hpd:
             start_head(h + 1)
+        if rest:
+            arrive(before(1, h))
 
         @pl.when(z + 1 < ctxs)
         def _():

time: 114 us -> 114 us (level)
  no operation moved by 1% of the time
where the time goes in v4:
time: 114 us; the launch traced here: 113 us
  Pallas kernels  109 us (96%)
  local copies, waits for them, and re-layouts  4.33 us (4%)
    pallas_call x1, Pallas kernels, local(): pl.pallas_call(functools.partial(kernel, heads, ctxs, rows, feat), out_sh...  109 us
    unnamed x6, local copies, waits for them, and re-layouts  4.33 us

profile of v4, /device:TPU:16, one launch (start us, length us, event | category | flops | bytes accessed | tf_op | source)
XLA Modules:
  0.0 113.4 jit_solution(2921316859199501871)
XLA Ops:
  0.0 0.8 copy.6.list_ref
  0.8 0.0 copy-start
  0.8 1.6 %copy-done = bf16[512,2048]{1,0:T(8,128)(2,1)S(1)} copy-done((bf16[512,2048]{1,0:T(8,128)(2,1)S(1)}, bf16[512,2048]{1,0:T(8,128)(2,1)}, u32[]{:S(2)}) %copy-start) | copy-done | bytes 2097176
  2.4 0.0 copy-start.1
  2.4 0.7 copy-done.1
  3.0 109.1 %shard_map.55 = bf16[512,2048]{1,0:T(8,128)(2,1)S(1)} custom-call(s32[2]{0:T(128)S(1)} %copy-done.1, s32[32,8]{1,0:T(8,128)S(1)} %copy.6.list_ref, bf16[512,2048]{1,0:T(8,128)(2,1)S(1)} %copy-done, bf16[512,2048]{1,0:T(8,128)(2,1)} %k_hbm.1, bf16[512,2048]{1,0:T(8,128)(2,1)} %v_hbm.1), custom_call_target="tpu_custom_call" | custom-call | tf_op jit(solution)/shard_map/pallas_call | solution.py:423
  112.1 1.3 %copy.8 = bf16[512,2048]{1,0:T(8,128)(2,1)} copy(bf16[512,2048]{1,0:T(8,128)(2,1)S(1)} %shard_map.55) | data formatting | bytes 4194304
Async XLA Ops:
  0.8 1.6 %copy-start = (bf16[512,2048]{1,0:T(8,128)(2,1)S(1)}, bf16[512,2048]{1,0:T(8,128)(2,1)}, u32[]{:S(2)}) copy-start(bf16[512,2048]{1,0:T(8,128)(2,1)} %q_hbm.1) | copy-start | bytes 6291460
  2.4 0.7 copy-start.1
